TPU v7x, 256 devices: a whole 4x4x8 slice. The times are simulated.
256 devices in a mesh: dp: 128 (over z, y, x), ep: 2 (over core).
Axes of the slice: x: 4, y: 4, z: 8, core: 2. Of those that a mesh axis runs over, the one named last changes fastest.
Arguments:
- queries: bfloat16 [2048, 64, 576], P('dp'), may hold values from -65 to 65
- latent_cache: bfloat16 [2048, 256, 576], P('dp', 'ep'), may hold values from -6 to 6
- cache_lens: int32 [2048], P('dp'), may hold values from 2 to 256
- movers: int32 [128, 4], P('dp'), may hold values from 0 to 16, as said below
- hidden: bfloat16 [2048, 7168], P('dp'), may hold values from -6 to 6
- norm_gain: float32 [7168], replicated, may hold values from 0.1 to 1.9
- routes: int32 [2048, 8], P('dp'), may hold values from 0 to 31, all different within a row; in each aligned block of 16 rows (0 to 15, 16 to 31, ...) at most 8 rows name the same one
- gate_weights: bfloat16 [2048, 8], P('dp'), may hold values from 0.19921875 to 1
- gate_proj: bfloat16 [128, 7168, 256], P('dp', None, 'ep'), may hold values from -0.0625 to 0.0625
- up_proj: bfloat16 [128, 7168, 256], P('dp', None, 'ep'), may hold values from -0.0625 to 0.0625
- down_proj: bfloat16 [128, 1024, 1792], P('dp', None, 'ep'), may hold values from -0.1875 to 0.1875
Outputs:
- served: bfloat16 [2560, 64, 512], P('dp', 'ep')
- expert_mix: bfloat16 [2048, 7168], P('dp', 'ep')
Inputs may be any that keep to these rules, and one draw needn't show every extreme that they name: `movers`: row i lists distinct request slots of rank i, followed by 16 in unused entries; a rank whose partner (i + 64) mod 128 lists any slot lists none itself. `routes`: each row names 8 different experts; among the 16 rows of one dp rank no expert is named more than 8 times.
All inputs are finite; a program needn't handle non-finite values.
Results may differ from a plain program's by a relative error of at most 0.015.
Values may be sent and summed in bfloat16 or wider, within the bound.
No kernel may reach another device: no remote copies, remote signals or barrier semaphores. Data moves between devices by JAX's collectives and lax.ppermute only.
A program may use at most 128 MiB of HBM per device.

v0:
```python
import jax
import jax.numpy as jnp
from jax import lax
from jax.sharding import PartitionSpec as P

LAT = 512


softmax_scale = 192 ** (-0.5)


def from_behind(x, axis, by):
    devices = lax.axis_size(axis)
    return lax.ppermute(x, axis, [(i, (i + by) % devices) for i in range(devices)])


def swapped(block, axis, distance):
    count = lax.axis_size(axis)
    route = []
    for low in range(count):
        high = low | 1 << distance
        if high != low and high < count:
            route += [(low, high), (high, low)]
    return lax.ppermute(block, axis, route)


def attend(queries, latent_cache, lengths):
    key_span = latent_cache.shape[1]
    offset = lax.axis_index("ep") * key_span
    scores = (
        jnp.einsum("shc,stc->sht", queries, latent_cache, preferred_element_type=jnp.float32)
        * softmax_scale
    )
    positions = offset + jnp.arange(key_span, dtype=jnp.int32)
    is_valid = positions[None, None, :] < lengths[:, None, None]
    masked = jnp.where(is_valid, scores, -1e30)
    local_peak = jnp.max(masked, axis=2)
    row_peak = lax.pmax(local_peak, "ep")
    weights = jnp.where(is_valid, jnp.exp(masked - row_peak[:, :, None]), 0.0)
    local_total = jnp.sum(weights, axis=2)
    numerator = jnp.einsum(
        "sht,stc->shc",
        weights.astype(jnp.bfloat16),
        latent_cache[:, :, :LAT],
        preferred_element_type=jnp.float32,
    )
    numerator, denominator = (
        lax.psum_scatter(
            numerator.astype(jnp.bfloat16), "ep", scatter_dimension=1, tiled=True
        ).astype(jnp.float32),
        lax.psum_scatter(
            local_total.astype(jnp.bfloat16), "ep", scatter_dimension=1, tiled=True
        ).astype(jnp.float32),
    )
    present = lengths[:, None, None] > 0
    divisor = jnp.where(present, denominator[:, :, None], 1.0)
    return jnp.where(present, numerator / divisor, 0.0).astype(jnp.bfloat16)


def local(
    queries,
    latent_cache,
    cache_lens,
    movers,
    hidden,
    norm_gain,
    routes,
    gate_weights,
    gate_proj,
    up_proj,
    down_proj,
):
    requests = queries.shape[0]
    listed = movers[0]
    in_use = listed < requests
    clamped = jnp.minimum(listed, requests - 1)
    slot_ids = jnp.arange(requests, dtype=jnp.int32)
    flagged = jnp.any(slot_ids[:, None] == listed[None, :], axis=1)
    partner_shift = lax.axis_size("dp") // 2
    outgoing_len = jnp.where(in_use, cache_lens[clamped], 0)
    arrived_cache, arrived_queries, arrived_len = from_behind(
        (latent_cache[clamped], queries[clamped], outgoing_len), "dp", partner_shift
    )
    served = attend(
        jnp.concatenate([queries, arrived_queries], axis=0),
        jnp.concatenate([latent_cache, arrived_cache], axis=0),
        jnp.concatenate([jnp.where(flagged, 0, cache_lens), arrived_len], axis=0),
    )
    rank_count = lax.axis_size("dp")
    core_count = lax.axis_size("ep")
    route_count = routes.shape[1]
    experts = max(route_count, rank_count // 4)
    group_size = rank_count // experts
    capacity = min(requests, 2 * requests * route_count // experts)
    model_width = hidden.shape[1]
    half_width = model_width // core_count
    core_index = lax.axis_index("ep")
    rank_index = lax.axis_index("dp")
    column_start = core_index * half_width
    widened = hidden.astype(jnp.float32)
    normed = (
        widened * lax.rsqrt(jnp.mean(widened * widened, axis=1, keepdims=True) + 1e-06) * norm_gain
    ).astype(jnp.bfloat16)
    flat_routes = routes.reshape(-1)
    onehot = (flat_routes[:, None] == jnp.arange(experts, dtype=jnp.int32)[None, :]).astype(
        jnp.int32
    )
    earlier = jnp.cumsum(onehot, axis=0) - onehot
    slot_index = jnp.sum(earlier * onehot, axis=1)
    target = (flat_routes * capacity + slot_index).reshape(requests, route_count)
    columns = jnp.arange(experts * capacity, dtype=jnp.int32)
    matches = target[:, :, None] == columns[None, None, :]
    placement = jnp.any(matches, axis=1).astype(jnp.bfloat16)
    combine = jnp.sum(
        jnp.where(matches, gate_weights[:, :, None].astype(jnp.float32), 0.0), axis=1
    ).astype(jnp.bfloat16)
    share_size = capacity // core_count
    chosen = lax.dynamic_index_in_dim(
        placement.reshape(requests, experts, core_count, share_size), core_index, 2, keepdims=False
    ).reshape(requests, experts * share_size)
    outbound = (
        jnp.einsum("rs,rd->sd", chosen, normed, preferred_element_type=jnp.float32)
        .astype(jnp.bfloat16)
        .reshape(experts, 1, share_size, model_width)
    )
    outbound = jnp.broadcast_to(outbound, (experts, group_size, share_size, model_width)).reshape(
        rank_count, share_size, model_width
    )
    arrived = lax.all_to_all(outbound, "dp", split_axis=0, concat_axis=0, tiled=True)
    gathered_rows = lax.all_gather(arrived, "ep", axis=1, tiled=True)
    stacked = gathered_rows.reshape(rank_count * capacity, model_width)
    gate_val = jnp.dot(stacked, gate_proj[0], preferred_element_type=jnp.float32)
    up_val = jnp.dot(stacked, up_proj[0], preferred_element_type=jnp.float32)
    activated = (jax.nn.silu(gate_val) * up_val).astype(jnp.bfloat16)
    joined = lax.all_gather(activated, "ep", axis=1, tiled=True)
    for bit_level in range(group_size.bit_length() - 1):
        partner_units = swapped(joined, "dp", bit_level)
        is_upper = rank_index // (1 << bit_level) % 2 == 1
        joined = jnp.where(
            is_upper,
            jnp.concatenate([partner_units, joined], axis=1),
            jnp.concatenate([joined, partner_units], axis=1),
        )
    expert_out = (
        jnp.dot(joined, down_proj[0], preferred_element_type=jnp.float32)
        .astype(jnp.bfloat16)
        .reshape(rank_count, capacity, -1)
    )
    returned = lax.all_to_all(expert_out, "dp", split_axis=0, concat_axis=0, tiled=True)
    weighted = jnp.einsum(
        "res,egsd->rgd",
        combine.reshape(requests, experts, capacity),
        returned.reshape(experts, group_size, capacity, -1),
        preferred_element_type=jnp.float32,
    ).reshape(requests, half_width)
    expert_mix = (lax.dynamic_slice_in_dim(widened, column_start, half_width, 1) + weighted).astype(
        jnp.bfloat16
    )
    return (served, expert_mix)


def solution(mesh):
    placed = (
        P("dp", None, None),
        P("dp", "ep", None),
        P("dp"),
        P("dp", None),
        P("dp", None),
        P(),
        P("dp", None),
        P("dp", None),
        P("dp", None, "ep"),
        P("dp", None, "ep"),
        P("dp", None, "ep"),
    )
    return jax.shard_map(
        local,
        mesh=mesh,
        in_specs=placed,
        out_specs=(P("dp", "ep", None), P("dp", "ep")),
        check_vma=False,
    )
```

profile of v0, /device:TPU:32, one launch (start us, length us, event | category | flops | bytes accessed | tf_op | source)
XLA Modules:
  0.0 391.6 jit_solution(14678679800838376078)
XLA Ops:
  9.0 1.1 multiply_reduce_fusion
  10.2 2.9 convolution_convert_fusion
  13.1 4.1 %broadcast_in_dim.91 = bf16[32,4,7168]{2,1,0:T(4,128)(2,1)} reshape(bf16[128,7168]{1,0:T(8,128)(2,1)} %convolution_convert_fusion) | data formatting | bytes 3670016 | tf_op jit(solution)/shard_map/broadcast_in_dim | solution.py:126
  17.2 6.7 %broadcast_in_dim.92 = bf16[32,4,4,7168]{3,2,1,0:T(4,128)(2,1)} broadcast(bf16[32,4,7168]{2,1,0:T(4,128)(2,1)} %broadcast_in_dim.91), dimensions={0,2,3} | broadcast | bytes 9175040 | tf_op jit(solution)/shard_map/broadcast_in_dim | solution.py:126
  23.9 178.9 %all_to_all.10 = bf16[128,4,7168]{2,1,0:T(4,128)(2,1)S(1)} all-to-all(bf16[128,4,7168]{2,1,0:T(4,128)(2,1)} %bitcast.53), channel_id=1, replica_groups=mesh['dp'=128,'ep'=2] {'dp'}, dimensions={0} | all-to-all | bytes 14680064 | tf_op jit(solution)/shard_map/all_to_all | solution.py:129
  202.8 5.1 %copy.53 = bf16[128,4,7168]{2,0,1:T(8,128)(2,1)} copy(bf16[128,4,7168]{2,1,0:T(4,128)(2,1)S(1)} %all_to_all.10) | data formatting | bytes 14680064 | tf_op jit(solution)/shard_map/all_to_all | solution.py:129
  207.9 28.3 %all-gather.2.cloned.1.call-done = bf16[128,8,7168]{2,0,1:T(8,128)(2,1)} async-done(((bf16[128,4,7168]{2,0,1:T(8,128)(2,1)}), bf16[128,8,7168]{2,0,1:T(8,128)(2,1)}) %all-gather.2.cloned.1.call-update) | async-done | bytes 14680080 | tf_op jit(solution)/shard_map/all_gather | solution.py:130
  236.3 15.6 %fusion.2 = f32[1024,128]{1,0:T(8,128)S(1)} fusion(bf16[128,8,7168]{2,0,1:T(8,128)(2,1)} %all-gather.2.cloned.1.call-done, bf16[1,7168,128]{2,1,0:T(8,128)(2,1)} %param.19), kind=kOutput, calls=%fused_computation.5 | convolution fusion | flops 1879048192 | bytes 17039360 | tf_op jit(solution)/shard_map/dot_general | solution.py:132
  251.9 7.9 %fusion.40 = bf16[1024,128]{1,0:T(8,128)(2,1)S(1)} fusion(bf16[1,7168,128]{2,1,0:T(8,128)(2,1)S(1)} %copy-done.5, bf16[128,8,7168]{2,0,1:T(8,128)(2,1)S(1)} %copy-done.4, f32[1024,128]{1,0:T(8,128)S(1)} %fusion.2), kind=kOutput, calls=%fused_computation.37 | convolution fusion | flops 1879834624 | bytes 17301504 | tf_op jit(solution)/shard_map/dot_general | solution.py:133
  259.8 2.2 all_gather.7
  262.0 1.5 collective-permute-start.3
  264.1 4.9 %collective-permute-start = (s32[4]{0:T(128)S(1)}, s32[4]{0:T(128)S(1)}, u32[]{:S(2)}, u32[]{:S(2)}) collective-permute-start(s32[4]{0:T(128)S(1)} %compare_select_fusion.1), channel_id=1, source_target_pairs={{0,128},{2,130},{4,132},{6,134},{8,136},{10,138},{12,140},{14,142}... | collective-permute-start | bytes 56 | tf_op jit(solution)/shard_map/ppermute | solution.py:14
  269.0 3.1 gather_fusion.2
  273.2 2.6 gather_fusion.1
  275.8 4.8 %collective-permute-start.1 = (bf16[4,64,576]{2,1,0:T(8,128)(2,1)}, bf16[4,64,576]{2,1,0:T(8,128)(2,1)}, u32[]{:S(2)}, u32[]{:S(2)}) collective-permute-start(bf16[4,64,576]{2,1,0:T(8,128)(2,1)} %gather_fusion.1), channel_id=1, source_target_pairs={{0,128},{2,130},{4,132},{6,134},{8,136},{10,138},{12,140},{14,142}... | collective-permute-start | bytes 884744 | tf_op jit(solution)/shard_map/ppermute | solution.py:14
  280.7 1.5 maximum_select_fusion.4
  282.1 3.0 collective-permute-start.4
  285.3 3.2 constant_dynamic-update-slice_fusion.1
  288.7 17.2 %collective-permute-done.2 = bf16[4,128,576]{1,2,0:T(8,128)(2,1)} collective-permute-done((bf16[4,128,576]{1,2,0:T(8,128)(2,1)}, bf16[4,128,576]{1,2,0:T(8,128)(2,1)}, u32[]{:S(2)}, u32[]{:S(2)}) %collective-permute-start.2) | collective-permute-done | bytes 589856 | tf_op jit(solution)/shard_map/ppermute | solution.py:14
  305.8 1.9 constant_dynamic-update-slice_fusion
  308.3 5.2 %convert_bitcast_fusion = bf16[128,8,896]{2,1,0:T(8,128)(2,1)} fusion(bf16[1,1024,896]{2,1,0:T(8,128)(2,1)S(1)} %copy-done, bf16[1024,512]{1,0:T(8,128)(2,1)S(1)} %maximum_select_fusion.4, bf16[1024,512]{1,0:T(8,128)(2,1)} %collective-permute-done.4, pred[]{:T(512)S(6)} %eq.63), kind=kOutput, calls=%fused_computation.27 | convolution fusion | flops 1889402880 | bytes 5767169 | tf_op jit(solution)/shard_map/dot_general | solution.py:145
  313.5 15.2 %all-to-all-start.1 = ((bf16[128,8,896]{2,1,0:T(8,128)(2,1)}), bf16[128,8,896]{2,1,0:T(8,128)(2,1)}, u32[]{:S(2)}, u32[]{:S(2)}) async-start(bf16[128,8,896]{2,1,0:T(8,128)(2,1)} %convert_bitcast_fusion), calls=%async_computation.2 | async-start | bytes 3670016 | tf_op jit(solution)/shard_map/all_to_all | solution.py:149
  328.8 3.1 fusion.62
  331.9 3.3 pmax.7
  336.5 3.9 %fusion.26 = bf16[20,64,512]{2,1,0:T(8,128)(2,1)} fusion(bf16[20,128,576]{1,2,0:T(8,128)(2,1)} %constant_dynamic-update-slice_fusion, f32[20,64,128]{2,1,0:T(8,128)S(1)} %get-tuple-element.5, f32[20,64]{1,0:T(8,128)S(1)} %pmax.7, pred[20,128]{1,0:T(8,128)(4,1)S(1)} %broadcast_compare_fusion), kind=kOutput, calls=%fused_computation.32 | convolution fusion | flops 168919040 | bytes 4595200 | tf_op jit(solution)/shard_map/sht,stc->shc/dot_general | solution.py:41
  340.8 9.8 %reduce-scatter.7.cloned.1.call-done = bf16[32,20]{1,0:T(8,128)(2,1)} async-done(((bf16[64,20]{1,0:T(8,128)(2,1)}), bf16[32,20]{1,0:T(8,128)(2,1)}) %reduce-scatter.7.cloned.1.call-update) | async-done | bytes 1296
  351.5 17.1 %reduce-scatter.5.cloned.1.call-done = bf16[20,32,512]{2,1,0:T(8,128)(2,1)} async-done(((bf16[20,64,512]{2,1,0:T(8,128)(2,1)}), bf16[20,32,512]{2,1,0:T(8,128)(2,1)}) %reduce-scatter.5.cloned.1.call-update) | async-done | bytes 655376 | tf_op jit(solution)/shard_map/reduce_scatter | solution.py:48
  368.6 2.2 select_convert_fusion
  370.8 4.2 %all-to-all-done.1 = bf16[128,8,896]{2,1,0:T(8,128)(2,1)} async-done(((bf16[128,8,896]{2,1,0:T(8,128)(2,1)}), bf16[128,8,896]{2,1,0:T(8,128)(2,1)}, u32[]{:S(2)}, u32[]{:S(2)}) %all-to-all-start.1) | async-done | bytes 1835040 | tf_op jit(solution)/shard_map/all_to_all | solution.py:149
  375.0 3.5 copy.75
  378.5 4.0 %dot_general.32 = bf16[3584,32,8]{0,1,2:T(8,128)(2,1)} reshape(bf16[4,896,32,8]{1,0,2,3:T(4,128)(2,1)} %bitcast.54) | data formatting | bytes 3670016 | tf_op jit(solution)/shard_map/res,egsd->rgd/dot_general | solution.py:150
  382.5 2.5 fusion.7
  (53 shorter events, 7.0 us)
Async XLA Ops:
  7.2 301.2 %copy-start = (bf16[1,1024,896]{2,1,0:T(8,128)(2,1)S(1)}, bf16[1,1024,896]{2,1,0:T(8,128)(2,1)}, u32[]{:S(2)}) copy-start(bf16[1,1024,896]{2,1,0:T(8,128)(2,1)} %param.21) | copy-start | bytes 5505028
  7.2 229.1 %all-gather.2.cloned.1.call-start = ((), (), s32[]{:S(2)}) async-start(), calls=%async_computation.5 | async-start | bytes 22020096 | tf_op jit(solution)/shard_map/all_gather | solution.py:130
  236.3 15.6 %copy-start.4 = (bf16[128,8,7168]{2,0,1:T(8,128)(2,1)S(1)}, bf16[128,8,7168]{2,0,1:T(8,128)(2,1)}, u32[]{:S(2)}) copy-start(bf16[128,8,7168]{2,0,1:T(8,128)(2,1)} %all-gather.2.cloned.1.call-done) | copy-start | bytes 44040196
  236.3 15.6 %copy-start.5 = (bf16[1,7168,128]{2,1,0:T(8,128)(2,1)S(1)}, bf16[1,7168,128]{2,1,0:T(8,128)(2,1)}, u32[]{:S(2)}) copy-start(bf16[1,7168,128]{2,1,0:T(8,128)(2,1)} %param.20) | copy-start | bytes 5505028
  251.9 11.5 %copy-start.6 = (s32[1,4]{1,0:T(1,128)S(1)}, s32[1,4]{1,0:T(1,128)}, u32[]{:S(2)}) copy-start(s32[1,4]{1,0:T(1,128)} %param.14) | copy-start | bytes 52
  251.9 11.5 %copy-start.1 = (s32[16]{0:T(128)S(1)}, s32[16]{0:T(128)}, u32[]{:S(2)}) copy-start(s32[16]{0:T(128)} %param.13) | copy-start | bytes 196
  262.0 18.7 %collective-permute-start.3 = (bf16[1024,256]{1,0:T(8,128)(2,1)S(1)}, bf16[1024,256]{1,0:T(8,128)(2,1)}, u32[]{:S(2)}, u32[]{:S(2)}) collective-permute-start(bf16[1024,256]{1,0:T(8,128)(2,1)S(1)} %all_gather.7), channel_id=1, source_target_pairs={{0,2},{2,0},{4,6},{6,4},{8,10},{10,8},{12,14},{14,12},{16,18},{18,... | collective-permute-start | bytes 1572872 | tf_op jit(solution)/shard_map/ppermute | solution.py:24
  264.1 24.4 %collective-permute-start = (s32[4]{0:T(128)S(1)}, s32[4]{0:T(128)S(1)}, u32[]{:S(2)}, u32[]{:S(2)}) collective-permute-start(s32[4]{0:T(128)S(1)} %compare_select_fusion.1), channel_id=1, source_target_pairs={{0,128},{2,130},{4,132},{6,134},{8,136},{10,138},{12,140},{14,142}... | collective-permute-start | bytes 56 | tf_op jit(solution)/shard_map/ppermute | solution.py:14
  272.1 33.7 %collective-permute-start.2 = (bf16[4,128,576]{1,2,0:T(8,128)(2,1)}, bf16[4,128,576]{1,2,0:T(8,128)(2,1)}, u32[]{:S(2)}, u32[]{:S(2)}) collective-permute-start(bf16[4,128,576]{1,2,0:T(8,128)(2,1)} %gather_fusion.2), channel_id=1, source_target_pairs={{0,128},{2,130},{4,132},{6,134},{8,136},{10,138},{12,140},{14,142}... | collective-permute-start | bytes 1769480 | tf_op jit(solution)/shard_map/ppermute | solution.py:14
  275.8 52.9 %collective-permute-start.1 = (bf16[4,64,576]{2,1,0:T(8,128)(2,1)}, bf16[4,64,576]{2,1,0:T(8,128)(2,1)}, u32[]{:S(2)}, u32[]{:S(2)}) collective-permute-start(bf16[4,64,576]{2,1,0:T(8,128)(2,1)} %gather_fusion.1), channel_id=1, source_target_pairs={{0,128},{2,130},{4,132},{6,134},{8,136},{10,138},{12,140},{14,142}... | collective-permute-start | bytes 884744 | tf_op jit(solution)/shard_map/ppermute | solution.py:14
  282.1 26.2 %collective-permute-start.4 = (bf16[1024,512]{1,0:T(8,128)(2,1)S(1)}, bf16[1024,512]{1,0:T(8,128)(2,1)}, u32[]{:S(2)}, u32[]{:S(2)}) collective-permute-start(bf16[1024,512]{1,0:T(8,128)(2,1)S(1)} %maximum_select_fusion.4), channel_id=1, source_target_pairs={{0,4},{4,0},{2,6},{6,2},{8,12},{12,8},{10,14},{14,10},{16,20},{20,... | collective-permute-start | bytes 3145736 | tf_op jit(solution)/shard_map/ppermute | solution.py:24
  313.5 61.5 %all-to-all-start.1 = ((bf16[128,8,896]{2,1,0:T(8,128)(2,1)}), bf16[128,8,896]{2,1,0:T(8,128)(2,1)}, u32[]{:S(2)}, u32[]{:S(2)}) async-start(bf16[128,8,896]{2,1,0:T(8,128)(2,1)} %convert_bitcast_fusion), calls=%async_computation.2 | async-start | bytes 3670016 | tf_op jit(solution)/shard_map/all_to_all | solution.py:149
  328.7 22.0 %reduce-scatter.7.cloned.1.call-start = ((), (), s32[]{:S(2)}) async-start(), calls=%async_computation.6 | async-start | bytes 24576
  336.4 4.0 %copy-start.2 = (bf16[16,7168]{1,0:T(8,128)(2,1)S(1)}, bf16[16,7168]{1,0:T(8,128)(2,1)}, u32[]{:S(2)}) copy-start(bf16[16,7168]{1,0:T(8,128)(2,1)} %param.15) | copy-start | bytes 688132
  336.4 4.1 %copy-start.3 = (bf16[16,8]{0,1:T(8,128)(2,1)S(1)}, bf16[16,8]{0,1:T(8,128)(2,1)}, u32[]{:S(2)}) copy-start(bf16[16,8]{0,1:T(8,128)(2,1)} %param.18) | copy-start | bytes 772
  336.4 32.2 %reduce-scatter.5.cloned.1.call-start = ((), (), s32[]{:S(2)}) async-start(), calls=%async_computation.4 | async-start | bytes 1966080 | tf_op jit(solution)/shard_map/reduce_scatter | solution.py:48
Sparse Core Ops, SparseCore 0:
  208.1 28.1 all-gather.1
  336.5 14.0 reduce-scatter.6
  353.2 15.3 reduce-scatter.4
where the time goes:
time: 392 us
  blocking collectives  184 us (47%)
  waiting for transfers between devices  77.3 us (20%)
  matrix products  41.1 us (10%)
  local copies, waits for them, and re-layouts  37.9 us (10%)
  starting transfers between devices  30.6 us (8%)
  between operations  13.9 us (4%)
  other arithmetic  6.32 us (2%)
    all_to_all x1, blocking collectives, local(): lax.all_to_all(outbound, 'dp', split_axis=0, concat_axis=0, tiled=True)  179 us
    all_gather x1, waiting for transfers between devices, local(): gathered_rows = lax.all_gather(arrived, 'ep', axis=1, tiled=True)  28.3 us
    ppermute x3, waiting for transfers between devices, from_behind(): lax.ppermute(x, axis, [(i, (i + by) % devices) for i in range(devices)])  17.2 us
    reduce_scatter x1, waiting for transfers between devices, attend(): lax.psum_scatter(numerator.astype(jnp.bfloat16), 'ep', scatter_dimension=...  17.1 us
    dot_general x1, matrix products, local(): jnp.dot(stacked, gate_proj[0], preferred_element_type=jnp.float32)  15.6 us
    all_to_all x1, starting transfers between devices, local(): lax.all_to_all(expert_out, 'dp', split_axis=0, concat_axis=0, tiled=True)  15.2 us
    ppermute x3, starting transfers between devices, from_behind(): lax.ppermute(x, axis, [(i, (i + by) % devices) for i in range(devices)])  10.8 us
    broadcast_in_dim x2, local copies, waits for them, and re-layouts, local(): jnp.broadcast_to(outbound, (experts, group_size, share_size, model_width))  10.8 us
  transfers between devices with their start and end apart: 9, of which 6 were waited for; matrix products, arithmetic and copies ran while one was open for 8% of the time, Pallas kernels for 0%

commit v1 on v0

v1 whole, which is shorter than its diff:
```python
import jax
import jax.numpy as jnp
from jax import lax
from jax.sharding import Mesh, PartitionSpec as P

LAT = 512
EXPERTS = 32
CAP = 8
PLANE = ("z", "y")
SOFTMAX_SCALE = 192 ** (-0.5)
CHUNKS = 2
BF = jnp.bfloat16
F32 = jnp.float32


def shifted(x, axis, by):
    devices = lax.axis_size(axis)
    return lax.ppermute(x, axis, [(i, (i + by) % devices) for i in range(devices)])


def attend(queries, latent_cache, lengths, core):
    span = latent_cache.shape[1]
    heads = queries.shape[1] // 2
    scores = jnp.einsum("shc,stc->sht", queries, latent_cache, preferred_element_type=F32)
    scores = scores * SOFTMAX_SCALE
    positions = core * span + jnp.arange(span, dtype=jnp.int32)
    valid = positions[None, None, :] < lengths[:, None, None]
    masked = jnp.where(valid, scores, -1e30)
    peak = jnp.max(masked, axis=2)
    weights = jnp.where(valid, jnp.exp(masked - peak[:, :, None]), 0.0)
    total = jnp.sum(weights, axis=2)
    numerator = jnp.einsum(
        "sht,stc->shc", weights.astype(BF), latent_cache[:, :, :LAT], preferred_element_type=F32
    )

    def mine(a):
        return lax.dynamic_slice_in_dim(a, core * heads, heads, 1)

    def other(a):
        return lax.dynamic_slice_in_dim(a, (1 - core) * heads, heads, 1)

    far_numerator = shifted(other(numerator).astype(BF), "ep", 1).astype(F32)
    far_stats = shifted(jnp.stack([other(peak), other(total)]), "ep", 1)
    near_peak, far_peak = mine(peak), far_stats[0]
    both = jnp.maximum(near_peak, far_peak)
    near_scale, far_scale = jnp.exp(near_peak - both), jnp.exp(far_peak - both)
    denominator = near_scale * mine(total) + far_scale * far_stats[1]
    combined = (
        near_scale[:, :, None] * mine(numerator) + far_scale[:, :, None] * far_numerator
    )
    return (combined / denominator[:, :, None]).astype(BF)


def local(
    queries,
    latent_cache,
    cache_lens,
    movers,
    hidden,
    norm_gain,
    routes,
    gate_weights,
    gate_proj,
    up_proj,
    down_proj,
):
    requests, model_width = hidden.shape
    half = model_width // 2
    core = lax.axis_index("ep")
    x_index = lax.axis_index("x")

    widened = hidden.astype(F32)
    inverse = lax.rsqrt(jnp.mean(widened * widened, axis=1, keepdims=True) + 1e-06)
    own_hidden = lax.dynamic_slice_in_dim(hidden, core * half, half, 1).astype(F32)
    own_gain = lax.dynamic_slice_in_dim(norm_gain, core * half, half, 0)
    normed = (own_hidden * inverse * own_gain).astype(BF)
    flat_routes = routes.reshape(-1)
    onehot = (flat_routes[:, None] == jnp.arange(EXPERTS, dtype=jnp.int32)[None, :]).astype(
        jnp.int32
    )
    earlier = jnp.cumsum(onehot, axis=0) - onehot
    slot_index = jnp.sum(earlier * onehot, axis=1)
    target = (flat_routes * CAP + slot_index).reshape(routes.shape)
    columns = jnp.arange(EXPERTS * CAP, dtype=jnp.int32)
    matches = target[:, :, None] == columns[None, None, :]
    placement = jnp.any(matches, axis=1).astype(BF)
    combine = jnp.sum(
        jnp.where(matches, gate_weights[:, :, None].astype(F32), 0.0), axis=1
    ).astype(BF)

    def swap_weights(w):
        far = lax.dynamic_slice_in_dim(w, (1 - core) * half, half, 0)
        return shifted(far, "ep", 1)

    near_gate = lax.dynamic_slice_in_dim(gate_proj[0], core * half, half, 0)
    near_up = lax.dynamic_slice_in_dim(up_proj[0], core * half, half, 0)
    mixed = jnp.concatenate(
        [near_gate, near_up, swap_weights(gate_proj[0]), swap_weights(up_proj[0])], axis=1
    )

    def down_rows(which):
        parts = []
        for by in range(4):
            source = (x_index - by) % 4
            parts.append(
                lax.dynamic_slice_in_dim(down_proj[0], source * 256 + which * 128, 128, 0)
            )
        return jnp.concatenate(parts, axis=0)

    near_down, far_down = down_rows(core), down_rows(1 - core)

    width = half // CHUNKS
    total = None
    attention = None
    for k in range(CHUNKS):
        part = normed[:, k * width : (k + 1) * width]
        outbound = jnp.einsum("rs,rd->sd", placement, part, preferred_element_type=F32)
        outbound = outbound.astype(BF).reshape(EXPERTS, CAP, width)
        arrived = lax.all_to_all(outbound, PLANE, split_axis=0, concat_axis=0, tiled=True)
        rows = lax.all_gather(arrived.reshape(EXPERTS * CAP, width), "x", axis=0, tiled=True)
        if k == CHUNKS - 1:
            attention = attend(queries, latent_cache, cache_lens, core)
            rows, attention = lax.optimization_barrier((rows, attention))
        product = jnp.dot(
            rows, mixed[k * width : (k + 1) * width], preferred_element_type=F32
        )
        total = product if total is None else total + product

    arrived = shifted(total[:, 256:], "ep", 1)
    value = total[:, :256] + arrived
    activated = (jax.nn.silu(value[:, :128]) * value[:, 128:]).astype(BF)
    blocks = [activated] + [shifted(activated, "x", by) for by in (1, 2, 3)]
    near = jnp.concatenate(blocks, axis=1)
    far = shifted(near, "ep", 1)
    expert_out = (
        jnp.dot(near, near_down, preferred_element_type=F32)
        + jnp.dot(far, far_down, preferred_element_type=F32)
    ).astype(BF)
    returned = lax.all_to_all(
        expert_out.reshape(4 * EXPERTS, CAP, -1),
        ("x",) + PLANE,
        split_axis=0,
        concat_axis=0,
        tiled=True,
    )
    weighted = jnp.einsum(
        "rk,qkd->rqd",
        combine,
        returned.reshape(4, EXPERTS * CAP, -1),
        preferred_element_type=F32,
    ).reshape(requests, half)
    expert_mix = (own_hidden + weighted).astype(BF)

    listed = movers[0]
    slot_ids = jnp.arange(requests, dtype=jnp.int32)
    flagged = jnp.any(slot_ids[:, None] == listed[None, :], axis=1)
    nothing = jnp.zeros((), BF)
    moved = jnp.where(
        (listed < requests)[:, None, None], attention[jnp.minimum(listed, requests - 1)], nothing
    )
    arrived_contexts = shifted(moved, "z", 4)
    served = jnp.concatenate(
        [jnp.where(flagged[:, None, None], nothing, attention), arrived_contexts], axis=0
    )
    return served, expert_mix


def solution(mesh):
    grid = Mesh(mesh.devices.reshape(8, 4, 4, 2), ("z", "y", "x", "ep"))
    dp = ("z", "y", "x")
    placed = (
        P(dp, None, None),
        P(dp, "ep", None),
        P(dp),
        P(dp, None),
        P(dp, None),
        P(),
        P(dp, None),
        P(dp, None),
        P(dp, None, "ep"),
        P(dp, None, "ep"),
        P(dp, None, "ep"),
    )
    return jax.shard_map(
        local,
        mesh=grid,
        in_specs=placed,
        out_specs=(P(dp, "ep", None), P(dp, "ep")),
        check_vma=False,
    )
```

time: 392 us -> 252 us (0.64)
  blocking collectives: 184 us -> 65.9 us
  local copies, waits for them, and re-layouts: 37.9 us -> 10.7 us
  waiting for transfers between devices: 77.3 us -> 101 us
  matrix products: 41.1 us -> 21.6 us
  starting transfers between devices: 30.6 us -> 23.5 us
  other arithmetic: 6.32 us -> 12.5 us
    all_to_all x1 -> x2, blocking collectives: 179 us -> 65.9 us  [local(): lax.all_to_all(outbound, PLANE, split_axis=0, concat_axis=0, tiled=True)]
    ppermute x5 -> x10, waiting for transfers between devices: 17.7 us -> 59.2 us  [shifted(): lax.ppermute(x, axis, [(i, (i + by) % devices) for i in range(devices)])]
    dot_general x6 -> x8, matrix products: 37.9 us -> 19.1 us  [the longest x2 9.42 us: local(): jnp.dot(rows, mixed[k * width:(k + 1) * width], preferred_element_type=F32)]
    reduce_scatter x1 -> x0, waiting for transfers between devices: 17.1 us -> none  [attend(): lax.psum_scatter(numerator.astype(jnp.bfloat16), 'ep', scatter_dimension=...]
    all_gather x1 -> x2, waiting for transfers between devices: 28.3 us -> 41.6 us  [local(): lax.all_gather(arrived.reshape(EXPERTS * CAP, width), 'x', axis=0, tiled=...]
    broadcast_in_dim x2 -> x0, local copies, waits for them, and re-layouts: 10.8 us -> none  [local(): jnp.broadcast_to(outbound, (experts, group_size, share_size, model_width))]
    unnamed x4 -> x2, waiting for transfers between devices: 9.86 us -> 0.03 us
    concatenate x0 -> x3, other arithmetic: none -> 5.28 us  [the longest x1 3.28 us: local(): jnp.concatenate([near_gate, near_up, swap_weights(gate_proj[0]), swap_wei...]
  transfers between devices with their start and end apart: 9 -> 13, of which waited for: 6 -> 8; matrix products, arithmetic and copies ran while one was open for 8% -> 9% of each run, Pallas kernels for 0% -> 0%
where the time goes in v1:
time: 252 us; the launch traced here: 250 us
  waiting for transfers between devices  101 us (40%)
  blocking collectives  65.9 us (26%)
  starting transfers between devices  23.5 us (9%)
  matrix products  21.6 us (9%)
  between operations  14.5 us (6%)
  other arithmetic  12.5 us (5%)
  local copies, waits for them, and re-layouts  10.7 us (4%)
    all_to_all x2, blocking collectives, local(): lax.all_to_all(outbound, PLANE, split_axis=0, concat_axis=0, tiled=True)  65.9 us
    ppermute x10, waiting for transfers between devices, shifted(): lax.ppermute(x, axis, [(i, (i + by) % devices) for i in range(devices)])  59.2 us
    all_gather x2, waiting for transfers between devices, local(): lax.all_gather(arrived.reshape(EXPERTS * CAP, width), 'x', axis=0, tiled=...  41.6 us
    all_to_all x1, starting transfers between devices, local(): lax.all_to_all(expert_out.reshape(4 * EXPERTS, CAP, -1), ('x',) + PLANE,...  13.4 us
    ppermute x10, starting transfers between devices, shifted(): lax.ppermute(x, axis, [(i, (i + by) % devices) for i in range(devices)])  10.1 us
    dot_general x2, matrix products, local(): jnp.dot(rows, mixed[k * width:(k + 1) * width], preferred_element_type=F32)  9.42 us
  transfers between devices with their start and end apart: 13, of which 8 were waited for; matrix products, arithmetic and copies ran while one was open for 9% of the time, Pallas kernels for 0%

profile of v1, /device:TPU:32, one launch (start us, length us, event | category | flops | bytes accessed | tf_op | source)
XLA Modules:
  0.0 249.6 jit_solution(14010149028995460363)
XLA Ops:
  7.2 1.2 multiply_reduce_fusion
  10.8 1.0 fusion.37
  12.2 36.0 %all_to_all.15 = bf16[32,8,1792]{2,1,0:T(8,128)(2,1)} all-to-all(bf16[32,8,1792]{2,1,0:T(8,128)(2,1)S(1)} %fusion.1), channel_id=1, replica_groups=mesh['z'=8,'y'=4,'x'=4,'ep'=2] {'z','y'}, dimensions={0} | all-to-all | bytes 1835008 | tf_op jit(solution)/shard_map/all_to_all | solution.py:119
  48.8 29.9 %all_to_all.16 = bf16[32,8,1792]{2,1,0:T(8,128)(2,1)} all-to-all(bf16[32,8,1792]{2,1,0:T(8,128)(2,1)S(1)} %fusion.2), channel_id=1, replica_groups=mesh['z'=8,'y'=4,'x'=4,'ep'=2] {'z','y'}, dimensions={0} | all-to-all | bytes 1835008 | tf_op jit(solution)/shard_map/all_to_all | solution.py:119
  78.7 1.4 dynamic-slice_bitcast_fusion.3
  80.8 1.3 dynamic-slice_bitcast_fusion.2
  82.3 2.5 %fusion.54 = (f32[16,64]{1,0:T(8,128)S(1)}, f32[16,64,128]{2,1,0:T(8,128)S(1)}) fusion(bf16[16,64,576]{2,1,0:T(8,128)(2,1)S(1)} %copy-done, bf16[16,128,576]{1,2,0:T(8,128)(2,1)} %param.12, pred[16,128]{1,0:T(8,128)(4,1)S(1)} %broadcast_compare_fusion), kind=kOutput, calls=%fused_computation.98 | convolution fusion | flops 151387136 | bytes 4069376 | tf_op jit(solution)/shard_map/shc,stc->sht/dot_general | solution.py:24
  84.8 0.9 fusion.3
  85.7 0.9 dynamic-slice_convert_fusion
  87.7 1.2 collective-permute-done
  89.0 2.1 divide_convert_fusion
  91.1 3.3 %pad_maximum_fusion = bf16[3584,512]{1,0:T(8,128)(2,1)} fusion(bf16[3584,128]{1,0:T(8,128)(2,1)} %collective-permute-done.4, bf16[3584,128]{1,0:T(8,128)(2,1)} %collective-permute-done.3, bf16[3584,128]{1,0:T(8,128)(2,1)S(1)} %copy-done.3, bf16[3584,128]{1,0:T(8,128)(2,1)S(1)} %copy-done.2), kind=kLoop, calls=%fused_computation.3 | loop fusion | flops 14680064 | bytes 7340032 | tf_op jit(solution)/shard_map/concatenate | solution.py:97
  94.4 4.7 %fusion.5 = f32[1024,512]{0,1:T(8,128)S(1)} fusion(bf16[1024,1792]{1,0:T(8,128)(2,1)} %all-gather.3.cloned.1.call-done, bf16[3584,512]{1,0:T(8,128)(2,1)} %pad_maximum_fusion), kind=kOutput, calls=%fused_computation.11 | convolution fusion | flops 1879048192 | bytes 7602176 | tf_op jit(solution)/shard_map/dot_general | solution.py:124
  99.1 41.6 %all-gather.5.cloned.1.call-done = bf16[1024,1792]{1,0:T(8,128)(2,1)} async-done(((bf16[256,1792]{1,0:T(8,128)(2,1)}), bf16[1024,1792]{1,0:T(8,128)(2,1)}) %all-gather.5.cloned.1.call-update) | async-done | bytes 3670032 | tf_op jit(solution)/shard_map/all_gather | solution.py:120
  140.8 4.7 %fusion.10 = f32[1024,512]{0,1:T(8,128)S(1)} fusion(f32[1024,512]{0,1:T(8,128)S(1)} %fusion.5, bf16[1024,1792]{1,0:T(8,128)(2,1)} %all-gather.5.cloned.1.call-done, bf16[3584,512]{1,0:T(8,128)(2,1)} %pad_maximum_fusion), kind=kOutput, calls=%fused_computation.16 | convolution fusion | flops 1879572480 | bytes 9699328 | tf_op jit(solution)/shard_map/dot_general | solution.py:124
  145.7 2.6 %collective-permute-done.5 = f32[1024,256]{0,1:T(8,128)S(1)} collective-permute-done((f32[1024,256]{0,1:T(8,128)S(1)}, f32[1024,256]{0,1:T(8,128)S(1)}, u32[]{:S(2)}, u32[]{:S(2)}) %collective-permute-start.5) | collective-permute-done | bytes 1048608 | tf_op jit(solution)/shard_map/ppermute | solution.py:18
  148.7 1.0 collective-permute-start.6
  149.7 1.8 collective-permute-start.7
  151.5 2.1 collective-permute-start.8
  153.6 10.6 %collective-permute-done.6 = bf16[1024,128]{0,1:T(8,128)(2,1)S(1)} collective-permute-done((bf16[1024,128]{0,1:T(8,128)(2,1)S(1)}, bf16[1024,128]{0,1:T(8,128)(2,1)S(1)}, u32[]{:S(2)}, u32[]{:S(2)}) %collective-permute-start.6) | collective-permute-done | bytes 262176 | tf_op jit(solution)/shard_map/ppermute | solution.py:18
  164.8 1.1 pad_maximum_fusion.1
  166.3 2.7 %collective-permute-done.9 = bf16[1024,512]{0,1:T(8,128)(2,1)} collective-permute-done((bf16[1024,512]{0,1:T(8,128)(2,1)}, bf16[1024,512]{0,1:T(8,128)(2,1)}, u32[]{:S(2)}, u32[]{:S(2)}) %collective-permute-start.9) | collective-permute-done | bytes 1048608 | tf_op jit(solution)/shard_map/ppermute | solution.py:18
  169.0 2.6 %fusion.21 = f32[1024,896]{1,0:T(8,128)S(1)} fusion(bf16[1024,512]{0,1:T(8,128)(2,1)} %collective-permute-done.9, bf16[128,896]{1,0:T(8,128)(2,1)S(1)} %get-tuple-element.15, bf16[128,896]{1,0:T(8,128)(2,1)S(1)} %get-tuple-element.16, bf16[128,896]{1,0:T(8,128)(2,1)S(1)} %get-tuple-element.10, bf16[128,896]{1,0:T(8,128)(2,1)S(1)} %get-tuple-element.11), kind=kOutput, calls=%fused_computation.30 | convolution fusion | flops 943194112 | bytes 5636096 | tf_op jit(solution)/shard_map/dot_general | solution.py:137
  171.6 2.6 %fusion.9 = bf16[128,8,896]{2,1,0:T(8,128)(2,1)} fusion(f32[1024,896]{1,0:T(8,128)S(1)} %fusion.21, bf16[128,896]{1,0:T(8,128)(2,1)S(1)} %get-tuple-element.12, bf16[128,896]{1,0:T(8,128)(2,1)S(1)} %get-tuple-element.13, bf16[128,896]{1,0:T(8,128)(2,1)S(1)} %get-tuple-element.14, bf16[128,896]{1,0:T(8,128)(2,1)S(1)} %get-tuple-element.9, ...), kind=kOutput, calls=%fused_computation.15 | convolution fusion | flops 949223424 | bytes 7471104 | tf_op jit(solution)/shard_map/dot_general | solution.py:136
  174.1 13.4 %all-to-all-start.2 = ((bf16[128,8,896]{2,1,0:T(8,128)(2,1)}), bf16[128,8,896]{2,1,0:T(8,128)(2,1)S(1)}, u32[]{:S(2)}, u32[]{:S(2)}) async-start(bf16[128,8,896]{2,1,0:T(8,128)(2,1)} %fusion.9), calls=%async_computation.2 | async-start | bytes 3670016 | tf_op jit(solution)/shard_map/all_to_all | solution.py:139
  187.9 1.6 gather_fusion
  189.6 4.6 %collective-permute-start.2 = (bf16[4,32,512]{2,1,0:T(8,128)(2,1)S(1)}, bf16[4,32,512]{2,1,0:T(8,128)(2,1)S(1)}, u32[]{:S(2)}, u32[]{:S(2)}) collective-permute-start(bf16[4,32,512]{2,1,0:T(8,128)(2,1)S(1)} %broadcast_select_fusion.1), channel_id=1, source_target_pairs={{0,128},{32,160},{64,192},{96,224},{128,0},{160,32},{192,64},{224,... | collective-permute-start | bytes 393224 | tf_op jit(solution)/shard_map/ppermute | solution.py:18
  194.1 1.1 broadcast_select_fusion
  195.3 41.4 %collective-permute-done.2 = bf16[4,32,512]{2,1,0:T(8,128)(2,1)S(1)} collective-permute-done((bf16[4,32,512]{2,1,0:T(8,128)(2,1)S(1)}, bf16[4,32,512]{2,1,0:T(8,128)(2,1)S(1)}, u32[]{:S(2)}, u32[]{:S(2)}) %collective-permute-start.2) | collective-permute-done | bytes 131104 | tf_op jit(solution)/shard_map/ppermute | solution.py:18
  236.7 0.9 pad_maximum_fusion.2
  237.6 2.4 copy.30
  240.0 2.7 %fusion = bf16[16,3584]{1,0:T(8,128)(2,1)} fusion(bf16[3584,256]{1,0:T(8,128)(2,1)} %bitcast.70, bf16[16,7168]{1,0:T(8,128)(2,1)S(1)} %copy-done.7, s32[]{:T(128)S(6)} %select_n.100, bf16[16,256]{1,0:T(8,128)(2,1)S(1)} %select_reduce_fusion), kind=kOutput, calls=%fused_computation.2 | convolution fusion | flops 29532160 | bytes 2072580 | tf_op jit(solution)/shard_map/rk,qkd->rqd/dot_general | solution.py:146
  (80 shorter events, 7.2 us)
Async XLA Ops:
  7.2 75.1 %copy-start = (bf16[16,64,576]{2,1,0:T(8,128)(2,1)S(1)}, bf16[16,64,576]{2,1,0:T(8,128)(2,1)}, u32[]{:S(2)}) copy-start(bf16[16,64,576]{2,1,0:T(8,128)(2,1)} %param.11) | copy-start | bytes 3538948
  7.2 87.2 %all-gather.3.cloned.1.call-start = ((), (), s32[]{:S(2)}) async-start(), calls=%async_computation.3 | async-start | bytes 4587520 | tf_op jit(solution)/shard_map/all_gather | solution.py:120
  48.3 30.4 %copy-start.4 = (bf16[1,7168,128]{2,1,0:T(8,128)(2,1)S(1)}, bf16[1,7168,128]{2,1,0:T(8,128)(2,1)}, u32[]{:S(2)}) copy-start(bf16[1,7168,128]{2,1,0:T(8,128)(2,1)} %param.19) | copy-start | bytes 5505028
  48.3 92.5 %all-gather.5.cloned.1.call-start = ((), (), s32[]{:S(2)}) async-start(), calls=%async_computation.4 | async-start | bytes 4587520 | tf_op jit(solution)/shard_map/all_gather | solution.py:120
  78.7 2.2 copy-start.5
  80.1 2.1 copy-start.15
  80.1 11.0 %collective-permute-start.3 = (bf16[3584,128]{1,0:T(8,128)(2,1)}, bf16[3584,128]{1,0:T(8,128)(2,1)}, u32[]{:S(2)}, u32[]{:S(2)}) collective-permute-start(bf16[3584,128]{1,0:T(8,128)(2,1)} %get-tuple-element.18), channel_id=1, source_target_pairs={{0,1},{1,0},{2,3},{3,2},{4,5},{5,4},{6,7},{7,6},{8,9},{9,8},{10,11... | collective-permute-start | bytes 2752520 | tf_op jit(solution)/shard_map/ppermute | solution.py:18
  82.2 8.9 %collective-permute-start.4 = (bf16[3584,128]{1,0:T(8,128)(2,1)}, bf16[3584,128]{1,0:T(8,128)(2,1)}, u32[]{:S(2)}, u32[]{:S(2)}) collective-permute-start(bf16[3584,128]{1,0:T(8,128)(2,1)} %get-tuple-element.20), channel_id=1, source_target_pairs={{0,1},{1,0},{2,3},{3,2},{4,5},{5,4},{6,7},{7,6},{8,9},{9,8},{10,11... | collective-permute-start | bytes 2752520 | tf_op jit(solution)/shard_map/ppermute | solution.py:18
  82.3 2.6 %copy-start.1 = (bf16[16,128,576]{1,2,0:T(8,128)(2,1)S(1)}, bf16[16,128,576]{1,2,0:T(8,128)(2,1)}, u32[]{:S(2)}) copy-start(bf16[16,128,576]{1,2,0:T(8,128)(2,1)} %param.12) | copy-start | bytes 7077892
  86.6 2.4 collective-permute-start.1
  87.6 1.2 collective-permute-start
  87.6 3.5 %copy-start.2 = (bf16[3584,128]{1,0:T(8,128)(2,1)S(1)}, bf16[3584,128]{1,0:T(8,128)(2,1)}, u32[]{:S(2)}) copy-start(bf16[3584,128]{1,0:T(8,128)(2,1)} %get-tuple-element.17) | copy-start | bytes 2752516
  87.7 3.5 %copy-start.3 = (bf16[3584,128]{1,0:T(8,128)(2,1)S(1)}, bf16[3584,128]{1,0:T(8,128)(2,1)}, u32[]{:S(2)}) copy-start(bf16[3584,128]{1,0:T(8,128)(2,1)} %get-tuple-element.19) | copy-start | bytes 2752516
  145.6 2.7 %collective-permute-start.5 = (f32[1024,256]{0,1:T(8,128)S(1)}, f32[1024,256]{0,1:T(8,128)S(1)}, u32[]{:S(2)}, u32[]{:S(2)}) collective-permute-start(f32[1024,256]{0,1:T(8,128)S(1)} %slice.53), channel_id=1, source_target_pairs={{0,1},{1,0},{2,3},{3,2},{4,5},{5,4},{6,7},{7,6},{8,9},{9,8},{10,11... | collective-permute-start | bytes 3145736 | tf_op jit(solution)/shard_map/ppermute | solution.py:18
  148.5 17.6 %copy-start.6 = (bf16[1,1024,896]{2,1,0:T(8,128)(2,1)S(1)}, bf16[1,1024,896]{2,1,0:T(8,128)(2,1)}, u32[]{:S(2)}) copy-start(bf16[1,1024,896]{2,1,0:T(8,128)(2,1)} %param.21) | copy-start | bytes 5505028
  148.7 15.4 %collective-permute-start.6 = (bf16[1024,128]{0,1:T(8,128)(2,1)S(1)}, bf16[1024,128]{0,1:T(8,128)(2,1)S(1)}, u32[]{:S(2)}, u32[]{:S(2)}) collective-permute-start(bf16[1024,128]{0,1:T(8,128)(2,1)S(1)} %fusion.29), channel_id=1, source_target_pairs={{0,2},{2,4},{4,6},{6,0},{1,3},{3,5},{5,7},{7,1},{8,10},{10,12},{12... | collective-permute-start | bytes 786440 | tf_op jit(solution)/shard_map/ppermute | solution.py:18
  149.7 14.4 %collective-permute-start.7 = (bf16[1024,128]{0,1:T(8,128)(2,1)S(1)}, bf16[1024,128]{0,1:T(8,128)(2,1)S(1)}, u32[]{:S(2)}, u32[]{:S(2)}) collective-permute-start(bf16[1024,128]{0,1:T(8,128)(2,1)S(1)} %fusion.29), channel_id=1, source_target_pairs={{0,4},{2,6},{4,0},{6,2},{1,5},{3,7},{5,1},{7,3},{8,12},{10,14},{12... | collective-permute-start | bytes 786440 | tf_op jit(solution)/shard_map/ppermute | solution.py:18
  151.5 13.3 %collective-permute-start.8 = (bf16[1024,128]{0,1:T(8,128)(2,1)S(1)}, bf16[1024,128]{0,1:T(8,128)(2,1)S(1)}, u32[]{:S(2)}, u32[]{:S(2)}) collective-permute-start(bf16[1024,128]{0,1:T(8,128)(2,1)S(1)} %fusion.29), channel_id=1, source_target_pairs={{0,6},{2,0},{4,2},{6,4},{1,7},{3,1},{5,3},{7,5},{8,14},{10,8},{12,... | collective-permute-start | bytes 786440 | tf_op jit(solution)/shard_map/ppermute | solution.py:18
  164.1 0.7 copy-start.8
  164.1 1.8 copy-start.10
  164.8 1.1 copy-start.12
  165.9 3.0 %collective-permute-start.9 = (bf16[1024,512]{0,1:T(8,128)(2,1)}, bf16[1024,512]{0,1:T(8,128)(2,1)}, u32[]{:S(2)}, u32[]{:S(2)}) collective-permute-start(bf16[1024,512]{0,1:T(8,128)(2,1)} %pad_maximum_fusion.1), channel_id=1, source_target_pairs={{0,1},{1,0},{2,3},{3,2},{4,5},{5,4},{6,7},{7,6},{8,9},{9,8},{10,11... | collective-permute-start | bytes 3145736 | tf_op jit(solution)/shard_map/ppermute | solution.py:18
  169.0 2.6 %copy-start.9 = (bf16[1024,128]{0,1:T(8,128)(2,1)S(1)}, bf16[1024,128]{0,1:T(8,128)(2,1)}, u32[]{:S(2)}) copy-start(bf16[1024,128]{0,1:T(8,128)(2,1)} %copy-done.8) | copy-start | bytes 786436
  169.0 2.6 %copy-start.11 = (bf16[1024,128]{0,1:T(8,128)(2,1)S(1)}, bf16[1024,128]{0,1:T(8,128)(2,1)}, u32[]{:S(2)}) copy-start(bf16[1024,128]{0,1:T(8,128)(2,1)} %copy-done.10) | copy-start | bytes 786436
  169.0 2.6 %copy-start.13 = (bf16[1024,128]{0,1:T(8,128)(2,1)S(1)}, bf16[1024,128]{0,1:T(8,128)(2,1)}, u32[]{:S(2)}) copy-start(bf16[1024,128]{0,1:T(8,128)(2,1)} %copy-done.12) | copy-start | bytes 786436
  174.1 13.4 %copy-start.14 = (bf16[16,8]{0,1:T(8,128)(2,1)S(1)}, bf16[16,8]{0,1:T(8,128)(2,1)}, u32[]{:S(2)}) copy-start(bf16[16,8]{0,1:T(8,128)(2,1)} %param.18) | copy-start | bytes 772
  174.1 13.5 %copy-start.16 = (s32[1,4]{1,0:T(1,128)S(1)}, s32[1,4]{1,0:T(1,128)}, u32[]{:S(2)}) copy-start(s32[1,4]{1,0:T(1,128)} %param.14) | copy-start | bytes 52
  174.1 63.5 %all-to-all-start.2 = ((bf16[128,8,896]{2,1,0:T(8,128)(2,1)}), bf16[128,8,896]{2,1,0:T(8,128)(2,1)S(1)}, u32[]{:S(2)}, u32[]{:S(2)}) async-start(bf16[128,8,896]{2,1,0:T(8,128)(2,1)} %fusion.9), calls=%async_computation.2 | async-start | bytes 3670016 | tf_op jit(solution)/shard_map/all_to_all | solution.py:139
  189.6 47.2 %collective-permute-start.2 = (bf16[4,32,512]{2,1,0:T(8,128)(2,1)S(1)}, bf16[4,32,512]{2,1,0:T(8,128)(2,1)S(1)}, u32[]{:S(2)}, u32[]{:S(2)}) collective-permute-start(bf16[4,32,512]{2,1,0:T(8,128)(2,1)S(1)} %broadcast_select_fusion.1), channel_id=1, source_target_pairs={{0,128},{32,160},{64,192},{96,224},{128,0},{160,32},{192,64},{224,... | collective-permute-start | bytes 393224 | tf_op jit(solution)/shard_map/ppermute | solution.py:18
  237.6 2.4 copy-start.7
Sparse Core Ops, SparseCore 0:
  48.4 43.7 all-gather.2
  94.0 46.7 all-gather.4
